TPU v7x, 32 devices: a whole 2x2x4 slice. The times are simulated.
32 devices in a mesh: dp: 16 (over z, x, core), tensor: 2 (over y).
Axes of the slice: x: 2, y: 2, z: 4, core: 2. Of those that a mesh axis runs over, the one named last changes fastest.
Arguments:
- inputs: bfloat16 [40960, 1024], P(('dp', 'tensor')), may hold values from -6 to 6
- teacher: bfloat16 [40960, 1024], P(('dp', 'tensor')), may hold values from -6 to 6
- lengths: int32 [128], replicated, may hold values from 200 to 320, as said below
- first_gain: float32 [1024], replicated, may hold values from 0.5 to 1.5
- first_shift: float32 [1024], replicated, may hold values from -0.2 to 0.2
- query_key_value_weight: bfloat16 [3, 1024, 1024], P(None, 'dp', 'tensor'), may hold values from -0.1875 to 0.1875
- heads_bias: float32 [2, 1024], P(None, 'tensor'), may hold values from -0.2 to 0.2
- merge_weight: bfloat16 [1024, 1024], P('dp', 'tensor'), may hold values from -1.5 to 1.5
- merge_bias: float32 [1024], replicated, may hold values from -0.6 to 0.6
- second_gain: float32 [1024], replicated, may hold values from 0.5 to 1.5
- second_shift: float32 [1024], replicated, may hold values from -0.6 to 0.6
- expand_weight: bfloat16 [1024, 4096], P('dp', 'tensor'), may hold values from -0.1875 to 0.1875
- expand_bias: float32 [4096], P('tensor'), may hold values from -0.6 to 0.6
- reduce_weight: bfloat16 [1024, 4096], P('dp', 'tensor'), may hold values from -0.09375 to 0.09375
- reduce_bias: float32 [1024], replicated, may hold values from -0.6 to 0.6
Outputs:
- loss_value: float32 [], replicated
- outputs: bfloat16 [40960, 1024], P(('dp', 'tensor'))
- inputs_grad: float32 [40960, 1024], P(('dp', 'tensor'))
- first_gain_grad: float32 [1024], replicated
- first_shift_grad: float32 [1024], replicated
- heads_weight_grad: float32 [3, 1024, 1024], P(None, 'dp', 'tensor')
- heads_bias_grad: float32 [2, 1024], P(None, 'tensor')
- merge_weight_grad: float32 [1024, 1024], P('dp', 'tensor')
- merge_bias_grad: float32 [1024], replicated
- second_gain_grad: float32 [1024], replicated
- second_shift_grad: float32 [1024], replicated
- expand_weight_grad: float32 [1024, 4096], P('dp', 'tensor')
- expand_bias_grad: float32 [4096], P('tensor')
- reduce_weight_grad: float32 [1024, 4096], P('dp', 'tensor')
- reduce_bias_grad: float32 [1024], replicated
Inputs may be any that keep to these rules, and one draw needn't show every extreme that they name: `lengths`: in every draw some image has all 320 slots valid.
All inputs are finite; a program needn't handle non-finite values.
Results may differ from a plain program's by a relative error of at most 0.0095.
Values may be sent and summed in bfloat16 or wider, within the bound.
A program may use at most 320 MiB of HBM per device.

v0:
```python
from functools import partial
import math
import jax
import jax.numpy as jnp
from jax import lax
from jax.sharding import PartitionSpec as P

HD = 64
SLOTS = 320
EPSILON = 1e-05
MASKED_SCORE = -1e30


def layer_norm(rows, gain, shift):
    centre = jnp.mean(rows, axis=-1, keepdims=True)
    centred = rows - centre
    spread = jnp.mean(centred * centred, axis=-1, keepdims=True)
    return centred * lax.rsqrt(spread + EPSILON) * gain + shift


def gather_rows(values):
    return lax.all_gather(values, "tensor", axis=0, tiled=True)


def reduce_rows(values):
    return lax.psum_scatter(values, "tensor", scatter_dimension=0, tiled=True)


def fetch_mixing(query_key_value_weight, merge_weight):
    return (
        lax.all_gather(query_key_value_weight, "dp", axis=1, tiled=True),
        lax.all_gather(merge_weight, "dp", axis=0, tiled=True),
    )


def fetch_feed(expand_weight, reduce_weight):
    return (
        lax.all_gather(expand_weight, "dp", axis=0, tiled=True),
        lax.all_gather(reduce_weight, "dp", axis=0, tiled=True),
    )


def masked_scores(query_heads, key_heads, key_valid, scale):
    raw_scores = (
        jnp.einsum("bqhe,bkhe->bhqk", query_heads, key_heads, preferred_element_type=jnp.float32)
        * scale
    )
    return jnp.where(key_valid[:, None, None, :], raw_scores, MASKED_SCORE)


def body(
    inputs,
    teacher,
    lengths,
    first_gain,
    first_shift,
    query_key_value_weight,
    heads_bias,
    merge_weight,
    merge_bias,
    second_gain,
    second_shift,
    expand_weight,
    expand_bias,
    reduce_weight,
    reduce_bias,
):
    local_rows = inputs.shape[0]
    group_rows = local_rows * lax.axis_size("tensor")
    images = group_rows // SLOTS
    local_width = query_key_value_weight.shape[2]
    local_heads = local_width // HD
    scale = 1.0 / math.sqrt(HD)
    mine = lax.dynamic_slice_in_dim(lengths, lax.axis_index("dp") * images, images)
    key_valid = jnp.arange(SLOTS, dtype=jnp.int32)[None, :] < mine[:, None]
    row_valid = lax.dynamic_slice_in_dim(
        key_valid.reshape(group_rows), lax.axis_index("tensor") * local_rows, local_rows
    )
    row_valid = row_valid.astype(jnp.float32)[:, None]
    count = jnp.sum(lengths).astype(jnp.float32)
    inputs_f = inputs.astype(jnp.float32)
    normalized_rows, first_back = jax.vjp(layer_norm, inputs_f, first_gain, first_shift)
    normed_b = normalized_rows.astype(jnp.bfloat16)
    normalized_complete = gather_rows(normed_b)
    heads_complete_rows, merge_full = fetch_mixing(query_key_value_weight, merge_weight)
    projected_heads = jnp.einsum(
        "xz,ezi->exi", normalized_complete, heads_complete_rows, preferred_element_type=jnp.float32
    )
    queries = (projected_heads[0] + heads_bias[0]).astype(jnp.bfloat16)
    key_rows = projected_heads[1].astype(jnp.bfloat16)
    value_rows = (projected_heads[2] + heads_bias[1]).astype(jnp.bfloat16)
    query_heads = queries.reshape(images, SLOTS, local_heads, HD)
    key_heads = key_rows.reshape(images, SLOTS, local_heads, HD)
    value_heads = value_rows.reshape(images, SLOTS, local_heads, HD)
    scores = masked_scores(query_heads, key_heads, key_valid, scale)
    highest = jnp.max(scores, axis=-1, keepdims=True)
    expo = jnp.exp(scores - highest)
    totals = jnp.sum(expo, axis=-1, keepdims=True)
    attend = expo / totals
    log_total = highest + jnp.log(totals)
    mixed = jnp.einsum(
        "bhqk,bkhe->bqhe",
        attend.astype(jnp.bfloat16),
        value_heads,
        preferred_element_type=jnp.float32,
    )
    mixed_b = mixed.reshape(group_rows, local_width).astype(jnp.bfloat16)
    branch_part = jnp.einsum("rf,df->rd", mixed_b, merge_full, preferred_element_type=jnp.float32)
    hidden_state = inputs_f + reduce_rows(branch_part) + merge_bias
    second, second_back = jax.vjp(layer_norm, hidden_state, second_gain, second_shift)
    second_b = second.astype(jnp.bfloat16)
    second_full = gather_rows(second_b)
    expand_full, reduce_full = fetch_feed(expand_weight, reduce_weight)
    pre_act = jnp.dot(second_full, expand_full, preferred_element_type=jnp.float32) + expand_bias
    activ, gelu_back = jax.vjp(partial(jax.nn.gelu, approximate=True), pre_act)
    activ_b = activ.astype(jnp.bfloat16)
    feed_part = jnp.einsum("rf,df->rd", activ_b, reduce_full, preferred_element_type=jnp.float32)
    feed_sum = reduce_rows(feed_part)
    result = (hidden_state + feed_sum + reduce_bias) * row_valid
    error = (result - teacher.astype(jnp.float32)) * row_valid
    loss_part = jnp.sum(error * error)
    result_grad = 2.0 * error / count
    expand_back, reduce_back = fetch_feed(expand_weight, reduce_weight)
    second_src = gather_rows(second_b)
    result_full = gather_rows(result_grad.astype(jnp.bfloat16))
    activ_grad = jnp.dot(result_full, reduce_back, preferred_element_type=jnp.float32)
    reduce_grad = jnp.einsum("rd,rf->df", result_full, activ_b, preferred_element_type=jnp.float32)
    pre_grad = gelu_back(activ_grad)[0].astype(jnp.bfloat16)
    expand_bias_grad = jnp.sum(pre_grad, axis=0, dtype=jnp.float32)
    expand_grad = jnp.einsum("rd,rf->df", second_src, pre_grad, preferred_element_type=jnp.float32)
    second_grad = reduce_rows(
        jnp.einsum("rf,df->rd", pre_grad, expand_back, preferred_element_type=jnp.float32)
    )
    hidden_ln_grad, second_gain_grad, second_shift_grad = second_back(second_grad)
    hidden_grad = result_grad + hidden_ln_grad
    reduce_bias_grad = jnp.sum(result_grad, axis=0)
    merge_bias_grad = jnp.sum(hidden_grad, axis=0)
    heads_pullback_rows, merge_back = fetch_mixing(query_key_value_weight, merge_weight)
    normalized_input_rows = gather_rows(normed_b)
    hidden_full = gather_rows(hidden_grad.astype(jnp.bfloat16))
    mixed_grad = jnp.einsum(
        "rd,df->rf", hidden_full, merge_back, preferred_element_type=jnp.float32
    ).astype(jnp.bfloat16)
    merge_grad = jnp.einsum("rd,rf->df", hidden_full, mixed_b, preferred_element_type=jnp.float32)
    mixed_heads = mixed_grad.reshape(images, SLOTS, local_heads, HD)
    attend_again = jnp.exp(masked_scores(query_heads, key_heads, key_valid, scale) - log_total)
    value_grad = jnp.einsum(
        "bhqk,bqhe->bkhe",
        attend_again.astype(jnp.bfloat16),
        mixed_heads,
        preferred_element_type=jnp.float32,
    ).astype(jnp.bfloat16)
    attend_grad = jnp.einsum(
        "bqhe,bkhe->bhqk", mixed_heads, value_heads, preferred_element_type=jnp.float32
    )
    score_grad = attend_again * (
        attend_grad - jnp.sum(attend_again * attend_grad, axis=-1, keepdims=True)
    )
    score_grad = score_grad.astype(jnp.bfloat16)
    query_grad = (
        jnp.einsum("bhqk,bkhe->bqhe", score_grad, key_heads, preferred_element_type=jnp.float32)
        * scale
    ).astype(jnp.bfloat16)
    key_grad = (
        jnp.einsum("bhqk,bqhe->bkhe", score_grad, query_heads, preferred_element_type=jnp.float32)
        * scale
    ).astype(jnp.bfloat16)
    projected_heads_gradient = jnp.stack(
        [
            query_grad.reshape(group_rows, local_width),
            key_grad.reshape(group_rows, local_width),
            value_grad.reshape(group_rows, local_width),
        ]
    )
    heads_bias_grad = jnp.stack(
        [
            jnp.sum(projected_heads_gradient[0], axis=0, dtype=jnp.float32),
            jnp.sum(projected_heads_gradient[2], axis=0, dtype=jnp.float32),
        ]
    )
    heads_grad = jnp.einsum(
        "jb,mjx->mbx",
        normalized_input_rows,
        projected_heads_gradient,
        preferred_element_type=jnp.float32,
    )
    normed_grad = reduce_rows(
        jnp.einsum(
            "mex,mwx->ew",
            projected_heads_gradient,
            heads_pullback_rows,
            preferred_element_type=jnp.float32,
        )
    )
    inputs_ln_grad, first_gain_grad, first_shift_grad = first_back(normed_grad)
    inputs_grad = hidden_grad + inputs_ln_grad
    heads_grad, merge_grad = (
        lax.psum_scatter(
            heads_grad.astype(jnp.bfloat16), "dp", scatter_dimension=1, tiled=True
        ).astype(jnp.float32),
        lax.psum_scatter(
            merge_grad.astype(jnp.bfloat16), "dp", scatter_dimension=0, tiled=True
        ).astype(jnp.float32),
    )
    expand_grad, reduce_grad = (
        lax.psum_scatter(
            expand_grad.astype(jnp.bfloat16), "dp", scatter_dimension=0, tiled=True
        ).astype(jnp.float32),
        lax.psum_scatter(
            reduce_grad.astype(jnp.bfloat16), "dp", scatter_dimension=0, tiled=True
        ).astype(jnp.float32),
    )
    heads_bias_grad, expand_bias_grad = lax.psum((heads_bias_grad, expand_bias_grad), "dp")
    summed = lax.psum(
        (
            first_gain_grad,
            first_shift_grad,
            second_gain_grad,
            second_shift_grad,
            merge_bias_grad,
            reduce_bias_grad,
            loss_part,
        ),
        ("dp", "tensor"),
    )
    loss_value = summed[6] / count
    return (
        loss_value,
        result.astype(jnp.bfloat16),
        inputs_grad,
        summed[0],
        summed[1],
        heads_grad,
        heads_bias_grad,
        merge_grad,
        summed[4],
        summed[2],
        summed[3],
        expand_grad,
        expand_bias_grad,
        reduce_grad,
        summed[5],
    )


def solution(mesh):
    return jax.shard_map(
        body,
        mesh=mesh,
        in_specs=(
            P(("dp", "tensor"), None),
            P(("dp", "tensor"), None),
            P(),
            P(),
            P(),
            P(None, "dp", "tensor"),
            P(None, "tensor"),
            P("dp", "tensor"),
            P(),
            P(),
            P(),
            P("dp", "tensor"),
            P("tensor"),
            P("dp", "tensor"),
            P(),
        ),
        out_specs=(
            P(),
            P(("dp", "tensor"), None),
            P(("dp", "tensor"), None),
            P(),
            P(),
            P(None, "dp", "tensor"),
            P(None, "tensor"),
            P("dp", "tensor"),
            P(),
            P(),
            P(),
            P("dp", "tensor"),
            P("tensor"),
            P("dp", "tensor"),
            P(),
        ),
        check_vma=False,
    )
```

profile of v0, /device:TPU:0, one launch (start us, length us, event | category | flops | bytes accessed | tf_op | source)
XLA Modules:
  0.0 1575.8 jit_solution(5867062736825207133)
XLA Ops:
  17.6 69.5 %all-gather.9.cloned.1.call-done = bf16[2560,1024]{1,0:T(8,128)(2,1)} async-done(((bf16[1280,1024]{1,0:T(8,128)(2,1)}), bf16[2560,1024]{1,0:T(8,128)(2,1)}) %all-gather.9.cloned.1.call-update) | async-done | bytes 5242896 | tf_op jit(solution)/shard_map/all_gather | solution.py:22
  87.2 47.4 %all-gather.11.cloned.1.call-done = bf16[3,1024,512]{2,1,0:T(8,128)(2,1)} async-done(((bf16[3,64,512]{2,1,0:T(8,128)(2,1)}), bf16[3,1024,512]{2,1,0:T(8,128)(2,1)}) %all-gather.11.cloned.1.call-update) | async-done | bytes 3145744 | tf_op jit(solution)/shard_map/all_gather | solution.py:31
  134.6 11.3 convolution_bitcast_fusion
  153.2 9.3 fusion.60
  168.4 7.4 squeeze.7
  175.8 7.4 reshape.163
  183.2 6.9 copy.71
  196.0 7.3 squeeze.8
  212.2 16.7 %fusion.13 = (f32[8,8,320]{2,1,0:T(8,128)S(1)}, f32[8,8,320,320]{2,3,1,0:T(8,128)}) fusion(pred[8,320]{1,0:T(8,128)(4,1)S(1)} %iota_compare_fusion, bf16[8,320,8,64]{1,3,2,0:T(8,128)(2,1)S(1)} %copy-done.6, bf16[8,320,8,64]{1,0,3,2:T(8,128)(2,1)} %add_convert_fusion), kind=kOutput, calls=%fused_computation.22 | convolution fusion | flops 858501120 | bytes 31541760 | tf_op jit(solution)/shard_map/bqhe,bkhe->bhqk/dot_general | solution.py:45
  228.9 14.1 fusion
  243.0 16.4 %convert_bitcast_fusion.2 = bf16[8,320,8,64]{1,3,2,0:T(8,128)(2,1)} fusion(f32[8,8,320]{2,1,0:T(8,128)S(1)} %fusion, f32[8,8,320]{2,1,0:T(8,128)S(1)} %get-tuple-element.91, f32[8,8,320,320]{2,3,1,0:T(8,128)} %get-tuple-element.92, pred[8,320]{1,0:T(8,128)(4,1)S(1)} %iota_compare_fusion, bf16[8,320,8,64]{1,0,3,2:T(8,128)(2,1)} %add_convert_fusion.1), kind=kOutput, calls=%fused_computation.69 | convolution fusion | flops 872939520 | bytes 31623680 | tf_op jit(solution)/shard_map/bhqk,bkhe->bqhe/dot_general | solution.py:101
  270.9 8.8 fusion.61
  280.4 120.2 %reduce-scatter.8.cloned.1.call-done = f32[1280,1024]{1,0:T(8,128)} async-done(((f32[2560,1024]{1,0:T(8,128)}), f32[1280,1024]{1,0:T(8,128)}) %reduce-scatter.8.cloned.1.call-update) | async-done | bytes 5242896 | tf_op jit(solution)/shard_map/reduce_scatter | solution.py:26
  409.3 43.9 %all-gather.17.cloned.1.call-done = bf16[1024,2048]{1,0:T(8,128)(2,1)} async-done(((bf16[64,2048]{1,0:T(8,128)(2,1)}), bf16[1024,2048]{1,0:T(8,128)(2,1)}) %all-gather.17.cloned.1.call-update) | async-done | bytes 4194320 | tf_op jit(solution)/shard_map/all_gather | solution.py:38
  453.2 69.1 %all-gather.15.cloned.1.call-done = bf16[2560,1024]{1,0:T(8,128)(2,1)} async-done(((bf16[1280,1024]{1,0:T(8,128)(2,1)}), bf16[2560,1024]{1,0:T(8,128)(2,1)}) %all-gather.15.cloned.1.call-update) | async-done | bytes 5242896 | tf_op jit(solution)/shard_map/all_gather | solution.py:22
  522.3 23.8 %multiply_convert_fusion.1 = (bf16[2560,2048]{1,0:T(8,128)(2,1)}, f32[2560,2048]{1,0:T(8,128)}) fusion(f32[2048]{0:T(1024)S(1)} %copy-done.43, bf16[2560,1024]{1,0:T(8,128)(2,1)} %all-gather.15.cloned.1.call-done, bf16[1024,2048]{1,0:T(8,128)(2,1)} %all-gather.17.cloned.1.call-done), kind=kOutput, calls=%fused_computation.18 | convolution fusion | flops 10789847040 | bytes 40902656 | tf_op jit(solution)/shard_map/dot_general | solution.py:114
  546.1 29.1 %all-gather.19.cloned.1.call-done = bf16[1024,2048]{1,0:T(8,128)(2,1)} async-done(((bf16[64,2048]{1,0:T(8,128)(2,1)}), bf16[1024,2048]{1,0:T(8,128)(2,1)}) %all-gather.19.cloned.1.call-update) | async-done | bytes 4194320 | tf_op jit(solution)/shard_map/all_gather | solution.py:39
  575.2 16.7 %fusion.62 = f32[2560,1024]{1,0:T(8,128)} fusion(bf16[2560,2048]{1,0:T(8,128)(2,1)} %get-tuple-element.93, bf16[1024,2048]{1,0:T(8,128)(2,1)} %all-gather.19.cloned.1.call-done), kind=kOutput, calls=%fused_computation.111 | convolution fusion | flops 10737418240 | bytes 25165824 | tf_op jit(solution)/shard_map/rf,df->rd/dot_general | solution.py:117
  594.0 118.4 %reduce-scatter.10.cloned.1.call-done = f32[1280,1024]{1,0:T(8,128)} async-done(((f32[2560,1024]{1,0:T(8,128)}), f32[1280,1024]{1,0:T(8,128)}) %reduce-scatter.10.cloned.1.call-update) | async-done | bytes 5242896 | tf_op jit(solution)/shard_map/reduce_scatter | solution.py:26
  712.4 6.3 fusion.54
  726.7 68.7 %all-gather.21.cloned.1.call-done = bf16[2560,1024]{1,0:T(8,128)(2,1)} async-done(((bf16[1280,1024]{1,0:T(8,128)(2,1)}), bf16[2560,1024]{1,0:T(8,128)(2,1)}) %all-gather.21.cloned.1.call-update) | async-done | bytes 5242896 | tf_op jit(solution)/shard_map/all_gather | solution.py:22
  795.3 29.0 %convert_reduce_fusion = (f32[2048]{0:T(1024)}, bf16[2560,2048]{1,0:T(8,128)(2,1)S(1)}) fusion(f32[2560,2048]{1,0:T(8,128)} %get-tuple-element.94, f32[2048]{0:T(1024)S(1)} %copy-done.43, bf16[2560,1024]{1,0:T(8,128)(2,1)} %all-gather.21.cloned.1.call-done, bf16[1024,2048]{1,0:T(8,128)(2,1)} %all-gather.19.cloned.1.call-done), kind=kOutput, calls=%fused_computation.17 | convolution fusion | flops 10858002432 | bytes 40910848 | tf_op jit(solution)/shard_map/dot_general | solution.py:126
  828.2 14.5 fusion.63
  842.8 122.0 %reduce-scatter.12.cloned.1.call-done = f32[1280,1024]{1,0:T(8,128)} async-done(((f32[2560,1024]{1,0:T(8,128)}), f32[1280,1024]{1,0:T(8,128)}) %reduce-scatter.12.cloned.1.call-update) | async-done | bytes 5242896 | tf_op jit(solution)/shard_map/reduce_scatter | solution.py:26
  980.0 17.0 %convolution_convert_fusion.1 = bf16[1024,2048]{1,0:T(8,128)(2,1)} fusion(bf16[2560,1024]{1,0:T(8,128)(2,1)} %all-gather.21.cloned.1.call-done, bf16[2560,2048]{1,0:T(8,128)(2,1)} %get-tuple-element.93), kind=kOutput, calls=%fused_computation.63 | convolution fusion | flops 10739515392 | bytes 19922944 | tf_op jit(solution)/shard_map/rd,rf->df/dot_general | solution.py:127
  997.2 16.8 %convolution_convert_fusion.2 = bf16[1024,2048]{1,0:T(8,128)(2,1)} fusion(bf16[2560,1024]{1,0:T(8,128)(2,1)} %all-gather.15.cloned.1.call-done, bf16[2560,2048]{1,0:T(8,128)(2,1)} %copy-done.47), kind=kOutput, calls=%fused_computation.64 | convolution fusion | flops 10739515392 | bytes 19922944 | tf_op jit(solution)/shard_map/rd,rf->df/dot_general | solution.py:130
  1014.3 34.4 %all-gather.23.cloned.1.call-done = bf16[2560,1024]{1,0:T(8,128)(2,1)} async-done(((bf16[1280,1024]{1,0:T(8,128)(2,1)}), bf16[2560,1024]{1,0:T(8,128)(2,1)}) %all-gather.23.cloned.1.call-update) | async-done | bytes 5242896 | tf_op jit(solution)/shard_map/all_gather | solution.py:22
  1058.9 7.2 copy.76
  1066.1 24.7 %multiply_reduce_fusion = (f32[8,8,320]{2,1,0:T(8,128)S(1)}, f32[8,8,320,320]{2,3,1,0:T(8,128)}) fusion(f32[8,8,320]{2,1,0:T(8,128)S(1)} %log_add_fusion, f32[8,8,320,320]{2,3,1,0:T(8,128)} %get-tuple-element.92, pred[8,320]{1,0:T(8,128)(4,1)S(1)} %iota_compare_fusion, bf16[8,320,8,64]{1,3,2,0:T(8,128)(2,1)} %copy.76, bf16[8,320,8,64]{1,0,3,2:T(8,128)(2,1)S(1)} %copy-done.11), kind=kOutput, calls=%fused_computation.1 | convolution fusion | flops 871608320 | bytes 57838080 | tf_op jit(solution)/shard_map/bqhe,bkhe->bhqk/dot_general | solution.py:153
  1090.9 26.7 %multiply_convert_fusion = bf16[8,8,320,320]{2,3,1,0:T(8,128)(2,1)} fusion(f32[8,8,320,320]{2,3,1,0:T(8,128)} %get-tuple-element.96, f32[8,8,320]{2,1,0:T(8,128)S(1)} %get-tuple-element.95, f32[8,8,320]{2,1,0:T(8,128)S(1)} %log_add_fusion, f32[8,8,320,320]{2,3,1,0:T(8,128)} %get-tuple-element.92, pred[8,320]{1,0:T(8,128)(4,1)S(1)} %iota_compare_fusion), kind=kLoop, calls=%fused_computation | loop fusion | flops 39321600 | bytes 65702400 | tf_op jit(solution)/shard_map/convert_element_type | solution.py:159
  1117.6 15.0 convert_reduce_fusion.2
  1132.6 6.9 copy.100
  1139.5 8.2 reshape.161
  1147.7 9.9 fusion.30
  1157.6 6.8 copy.99
  1164.4 8.0 reshape.160
  1172.4 10.3 convert_reduce_fusion.3
  1182.7 6.7 copy.98
  1189.5 8.0 reshape.159
  1203.4 8.8 convert_bitcast_fusion
  1218.2 7.3 convolution_convert_fusion.3
  1225.7 13.0 convolution_bitcast_fusion.1
  1244.4 61.5 %all-reduce.2 = (f32[2,512]{1,0:T(2,128)}, f32[2048]{0:T(1024)}) all-reduce(f32[2,512]{1,0:T(2,128)S(1)} %pad_maximum_fusion, f32[2048]{0:T(1024)S(1)} %copy-done.35), channel_id=1, replica_groups=mesh['dp'=16,'tensor'=2] {'dp'}, use_global_device_ids=true, to_apply=%region_25.26 | all-reduce | flops 3072 | bytes 24576 | tf_op jit(solution)/shard_map/psum | solution.py:213
  1305.9 24.2 %all-reduce.5.cloned.1.call-done = bf16[3,1024,512]{2,0,1:T(4,128)(2,1)} async-done(((bf16[3,1024,512]{2,0,1:T(4,128)(2,1)}), bf16[3,1024,512]{2,0,1:T(4,128)(2,1)}) %all-reduce.5.cloned.1.call-update) | async-done | bytes 3145744
  1332.0 58.4 %reduce-scatter.16.cloned.1.call-done = bf16[64,512]{1,0:T(8,128)(2,1)} async-done(((bf16[1024,512]{1,0:T(8,128)(2,1)}), bf16[64,512]{1,0:T(8,128)(2,1)}) %reduce-scatter.16.cloned.1.call-update) | async-done | bytes 65552 | tf_op jit(solution)/shard_map/reduce_scatter | solution.py:201
  1391.9 121.6 %reduce-scatter.14.cloned.1.call-done = f32[1280,1024]{1,0:T(8,128)} async-done(((f32[2560,1024]{1,0:T(8,128)}), f32[1280,1024]{1,0:T(8,128)}) %reduce-scatter.14.cloned.1.call-update) | async-done | bytes 5242896 | tf_op jit(solution)/shard_map/reduce_scatter | solution.py:26
  1520.6 40.2 %all-reduce.1 = (f32[]{:T(128)}, f32[1024]{0:T(1024)}, f32[1024]{0:T(1024)}, f32[1024]{0:T(1024)}, f32[1024]{0:T(1024)}, /*index=5*/f32[1024]{0:T(1024)}, f32[1024]{0:T(1024)}) all-reduce(f32[]{:T(128)} %get-tuple-element.90, f32[1024]{0:T(1024)S(1)} %get-tuple-element.62, ...), channel_id=1, replica_groups=mesh['dp'=16,'tensor'=2] {'dp','tensor'}, use_global_device_ids=true, to_apply=%region_9.10 | all-reduce | flops 6145 | bytes 49160 | tf_op jit(solution)/shard_map/psum | solution.py:214
  1561.4 6.5 add_add_fusion.2
  (194 shorter events, 125.2 us)
Async XLA Ops:
  7.2 6.2 copy-start.1
  7.2 6.2 copy-start.28
  7.2 6.2 copy-start.36
  7.2 80.0 %all-gather.9.cloned.1.call-start = ((), (), s32[]{:S(2)}) async-start(), calls=%async_computation.7 | async-start | bytes 7864320 | tf_op jit(solution)/shard_map/all_gather | solution.py:22
  9.6 7.7 copy-start.44
  9.6 7.9 copy-start.40
  15.8 118.8 %all-gather.11.cloned.1.call-start = ((), (), s32[]{:S(2)}) async-start(), calls=%async_computation.8 | async-start | bytes 3342336 | tf_op jit(solution)/shard_map/all_gather | solution.py:31
  16.5 254.4 %all-gather.13.cloned.1.call-start = ((), (), s32[]{:S(2)}) async-start(), calls=%async_computation.9 | async-start | bytes 1114112 | tf_op jit(solution)/shard_map/all_gather | solution.py:32
  17.2 383.4 %reduce-scatter.8.cloned.1.call-start = ((), (), s32[]{:S(2)}) async-start(), calls=%async_computation.10 | async-start | bytes 15728640 | tf_op jit(solution)/shard_map/reduce_scatter | solution.py:26
  145.9 5.5 copy-start.13
  203.4 5.8 copy-start.9
  228.9 14.1 copy-start.17
  243.0 16.5 %copy-start.20 = (f32[8,8,320]{2,1,0:T(8,128)}, f32[8,8,320]{2,1,0:T(8,128)S(1)}, u32[]{:S(2)}) copy-start(f32[8,8,320]{2,1,0:T(8,128)S(1)} %fusion) | copy-start | bytes 245764
  279.7 120.9 %copy-start.37 = (f32[1024]{0:T(1024)S(1)}, f32[1024]{0:T(1024)}, u32[]{:S(2)}) copy-start(f32[1024]{0:T(1024)} %param.23) | copy-start | bytes 12292
  279.8 173.5 %all-gather.17.cloned.1.call-start = ((), (), s32[]{:S(2)}) async-start(), calls=%async_computation.12 | async-start | bytes 4456448 | tf_op jit(solution)/shard_map/all_gather | solution.py:38
  280.4 241.9 %all-gather.15.cloned.1.call-start = ((), (), s32[]{:S(2)}) async-start(), calls=%async_computation.11 | async-start | bytes 7864320 | tf_op jit(solution)/shard_map/all_gather | solution.py:22
  406.2 116.1 %copy-start.43 = (f32[2048]{0:T(1024)S(1)}, f32[2048]{0:T(1024)}, u32[]{:S(2)}) copy-start(f32[2048]{0:T(1024)} %param.27) | copy-start | bytes 24580
  408.5 166.7 %all-gather.19.cloned.1.call-start = ((), (), s32[]{:S(2)}) async-start(), calls=%async_computation.13 | async-start | bytes 4456448 | tf_op jit(solution)/shard_map/all_gather | solution.py:39
  409.2 303.2 %reduce-scatter.10.cloned.1.call-start = ((), (), s32[]{:S(2)}) async-start(), calls=%async_computation.14 | async-start | bytes 15728640 | tf_op jit(solution)/shard_map/reduce_scatter | solution.py:26
  591.9 120.6 %copy-start.39 = (f32[1024]{0:T(1024)S(1)}, f32[1024]{0:T(1024)}, u32[]{:S(2)}) copy-start(f32[1024]{0:T(1024)} %param.29) | copy-start | bytes 12292
  591.9 203.4 %all-gather.21.cloned.1.call-start = ((), (), s32[]{:S(2)}) async-start(), calls=%async_computation.15 | async-start | bytes 7864320 | tf_op jit(solution)/shard_map/all_gather | solution.py:22
  594.0 124.8 %copy-start.16 = (bf16[1280,1024]{1,0:T(8,128)(2,1)S(1)}, bf16[1280,1024]{1,0:T(8,128)(2,1)}, u32[]{:S(2)}) copy-start(bf16[1280,1024]{1,0:T(8,128)(2,1)} %param.16) | copy-start | bytes 7864324
  726.6 238.1 %reduce-scatter.12.cloned.1.call-start = ((), (), s32[]{:S(2)}) async-start(), calls=%async_computation.16 | async-start | bytes 15728640 | tf_op jit(solution)/shard_map/reduce_scatter | solution.py:26
  795.3 32.8 %copy-start.41 = (bf16[1024,2048]{1,0:T(8,128)(2,1)S(1)}, bf16[1024,2048]{1,0:T(8,128)(2,1)}, u32[]{:S(2)}) copy-start(bf16[1024,2048]{1,0:T(8,128)(2,1)} %all-gather.17.cloned.1.call-done) | copy-start | bytes 12582916
  842.7 206.0 %all-gather.23.cloned.1.call-start = ((), (), s32[]{:S(2)}) async-start(), calls=%async_computation.17 | async-start | bytes 7864320 | tf_op jit(solution)/shard_map/all_gather | solution.py:22
  964.7 5.8 copy-start.10
  964.7 9.7 slice-start
  980.0 17.2 %copy-start.18 = (f32[8,8,320]{2,1,0:T(8,128)S(1)}, f32[8,8,320]{2,1,0:T(8,128)}, u32[]{:S(2)}) copy-start(f32[8,8,320]{2,1,0:T(8,128)} %copy-done.17) | copy-start | bytes 245764
  980.0 17.2 %copy-start.21 = (f32[8,8,320]{2,1,0:T(8,128)S(1)}, f32[8,8,320]{2,1,0:T(8,128)}, u32[]{:S(2)}) copy-start(f32[8,8,320]{2,1,0:T(8,128)} %copy-done.20) | copy-start | bytes 245764
  980.0 260.6 %reduce-scatter.20.cloned.1.call-start = ((), (), s32[]{:S(2)}) async-start(), calls=%async_computation.21 | async-start | bytes 4456448 | tf_op jit(solution)/shard_map/reduce_scatter | solution.py:209
  997.1 245.3 %reduce-scatter.18.cloned.1.call-start = ((), (), s32[]{:S(2)}) async-start(), calls=%async_computation.20 | async-start | bytes 4456448 | tf_op jit(solution)/shard_map/reduce_scatter | solution.py:206
  1014.1 316.1 %all-reduce.5.cloned.1.call-start = ((), (), s32[]{:S(2)}) async-start(), calls=%async_computation.22 | async-start | bytes 8388608
  1058.9 7.2 copy-start.11
  1090.9 26.7 %copy-start.12 = (bf16[8,320,8,64]{1,3,2,0:T(8,128)(2,1)S(1)}, bf16[8,320,8,64]{1,3,2,0:T(8,128)(2,1)}, u32[]{:S(2)}) copy-start(bf16[8,320,8,64]{1,3,2,0:T(8,128)(2,1)} %copy.76) | copy-start | bytes 7864324
  1139.5 8.2 copy-start.8
  1164.4 8.0 copy-start.7
  1189.5 10.1 copy-start.15
  1197.5 5.9 slice-start.2
  1218.0 7.7 copy-start.42
  1218.0 172.4 %reduce-scatter.16.cloned.1.call-start = ((), (), s32[]{:S(2)}) async-start(), calls=%async_computation.19 | async-start | bytes 1114112 | tf_op jit(solution)/shard_map/reduce_scatter | solution.py:201
  1225.6 287.9 %reduce-scatter.14.cloned.1.call-start = ((), (), s32[]{:S(2)}) async-start(), calls=%async_computation.18 | async-start | bytes 15728640 | tf_op jit(solution)/shard_map/reduce_scatter | solution.py:26
  1238.7 5.7 copy-start.35
  1238.7 274.8 %copy-start.2 = (bf16[1280,1024]{1,0:T(8,128)(2,1)S(1)}, bf16[1280,1024]{1,0:T(8,128)(2,1)}, u32[]{:S(2)}) copy-start(bf16[1280,1024]{1,0:T(8,128)(2,1)} %param.15) | copy-start | bytes 7864324
  1238.7 274.8 %copy-start.23 = (f32[1280]{0:T(1024)S(1)}, f32[1280]{0:T(1024)}, u32[]{:S(2)}) copy-start(f32[1280]{0:T(1024)} %copy-done.22) | copy-start | bytes 15364
  1238.7 274.8 %copy-start.29 = (f32[1024]{0:T(1024)S(1)}, f32[1024]{0:T(1024)}, u32[]{:S(2)}) copy-start(f32[1024]{0:T(1024)} %param.18) | copy-start | bytes 12292
  1242.4 275.0 %copy-start.27 = (f32[1280]{0:T(1024)S(1)}, f32[1280]{0:T(1024)}, u32[]{:S(2)}) copy-start(f32[1280]{0:T(1024)} %copy-done.26) | copy-start | bytes 15364
  1242.4 275.0 %copy-start.25 = (f32[1280]{0:T(1024)S(1)}, f32[1280]{0:T(1024)}, u32[]{:S(2)}) copy-start(f32[1280]{0:T(1024)} %copy-done.24) | copy-start | bytes 15364
  1513.5 4.0 copy-start.4
  (20 other events, 50.7 us)
Sparse Core Ops, SparseCore 0:
  15.9 71.2 all-gather.8
  89.4 45.1 all-gather.10
  136.8 36.7 all-gather.12
  279.9 120.7 reduce-scatter.7
  402.7 50.5 all-gather.16
  455.2 67.0 all-gather.14
  524.5 50.7 all-gather.18
  592.0 120.3 reduce-scatter.9
  726.7 68.5 all-gather.20
  842.8 121.8 reduce-scatter.11
  980.1 68.5 all-gather.22
  1052.4 72.4 reduce-scatter.19
  1129.2 71.3 reduce-scatter.17
  1218.1 111.9 all-reduce.4
  1334.0 56.3 reduce-scatter.15
  1392.5 120.8 reduce-scatter.13
where the time goes:
time: 1590 us; the launch traced here: 1580 us
  waiting for transfers between devices  930 us (58%)
  matrix products  266 us (17%)
  local copies, waits for them, and re-layouts  154 us (10%)
  other arithmetic  105 us (7%)
  blocking collectives  102 us (6%)
  between operations  17.8 us (1%)
    reduce_scatter x4, waiting for transfers between devices, reduce_rows(): return lax.psum_scatter(values, 'tensor', scatter_dimension=0, tiled=True)  482 us
    all_gather x4, waiting for transfers between devices, gather_rows(): return lax.all_gather(values, 'tensor', axis=0, tiled=True)  242 us
    psum x1, blocking collectives, body(): lax.psum((heads_bias_grad, expand_bias_grad), 'dp')  61.5 us
    reduce_scatter x1, waiting for transfers between devices, body(): lax.psum_scatter(merge_grad.astype(jnp.bfloat16), 'dp', scatter_dimension...  58.4 us
    all_gather x1, waiting for transfers between devices, fetch_mixing(): lax.all_gather(query_key_value_weight, 'dp', axis=1, tiled=True)  47.4 us
    another operation x7, local copies, waits for them, and re-layouts, body(): jnp.stack([query_grad.reshape(group_rows, local_width), key_grad.reshape(...  44.8 us
    all_gather x1, waiting for transfers between devices, fetch_feed(): lax.all_gather(expand_weight, 'dp', axis=0, tiled=True)  43.9 us
    psum x1, blocking collectives, body(): lax.psum((first_gain_grad, first_shift_grad, second_gain_grad, second_shi...  40.2 us
  transfers between devices with their start and end apart: 16, of which 13 were waited for; matrix products, arithmetic and copies ran while one was open for 25% of the time, Pallas kernels for 0%

commit v1 on v0

--- a/solution.py
+++ b/solution.py
@@ -11,6 +11,18 @@
 MASKED_SCORE = -1e30
 
 
+def doubled_up(x, axis, dim):
+    ways, here = (lax.axis_size(axis), lax.axis_index(axis))
+    grown, reach = (x, 1)
+    while reach < ways:
+        theirs = lax.ppermute(grown, axis, [(d, d ^ reach) for d in range(ways)])
+        mine_first = jnp.concatenate([grown, theirs], axis=dim)
+        theirs_first = jnp.concatenate([theirs, grown], axis=dim)
+        grown = jnp.where(here & reach == 0, mine_first, theirs_first)
+        reach = 2 * reach
+    return grown
+
+
 def layer_norm(rows, gain, shift):
     centre = jnp.mean(rows, axis=-1, keepdims=True)
     centred = rows - centre
@@ -28,7 +40,7 @@
 
 def fetch_mixing(query_key_value_weight, merge_weight):
     return (
-        lax.all_gather(query_key_value_weight, "dp", axis=1, tiled=True),
+        doubled_up(query_key_value_weight, "dp", 1),
         lax.all_gather(merge_weight, "dp", axis=0, tiled=True),
     )
 

time: 1590 us -> 1550 us (0.975)
  local copies, waits for them, and re-layouts: 154 us -> 123 us
  waiting for transfers between devices: 930 us -> 906 us
  matrix products: 266 us -> 285 us
    ppermute x0 -> x4, waiting for transfers between devices: none -> 96.5 us  [doubled_up(): theirs = lax.ppermute(grown, axis, [(d, d ^ reach) for d in range(ways)])]
    all_gather x4, waiting for transfers between devices: 242 us -> 172 us  [gather_rows(): return lax.all_gather(values, 'tensor', axis=0, tiled=True)]
    all_gather x1 -> x0, waiting for transfers between devices: 47.4 us -> none  [fetch_mixing(): lax.all_gather(query_key_value_weight, 'dp', axis=1, tiled=True)]
  transfers between devices with their start and end apart: 16 -> 19, of which waited for: 13 -> 15; matrix products, arithmetic and copies ran while one was open for 25% -> 25% of each run, Pallas kernels for 0% -> 0%
where the time goes in v1:
time: 1550 us
  waiting for transfers between devices  906 us (58%)
  matrix products  285 us (18%)
  local copies, waits for them, and re-layouts  123 us (8%)
  other arithmetic  104 us (7%)
  blocking collectives  102 us (7%)
  between operations  17.9 us (1%)
    reduce_scatter x4, waiting for transfers between devices, reduce_rows(): return lax.psum_scatter(values, 'tensor', scatter_dimension=0, tiled=True)  484 us
    all_gather x4, waiting for transfers between devices, gather_rows(): return lax.all_gather(values, 'tensor', axis=0, tiled=True)  172 us
    ppermute x4, waiting for transfers between devices, doubled_up(): theirs = lax.ppermute(grown, axis, [(d, d ^ reach) for d in range(ways)])  96.5 us
    psum x1, blocking collectives, body(): lax.psum((heads_bias_grad, expand_bias_grad), 'dp')  61.5 us
    reduce_scatter x1, waiting for transfers between devices, body(): lax.psum_scatter(merge_grad.astype(jnp.bfloat16), 'dp', scatter_dimension...  58.4 us
    all_gather x1, waiting for transfers between devices, fetch_feed(): lax.all_gather(expand_weight, 'dp', axis=0, tiled=True)  44.1 us
    another operation x7, local copies, waits for them, and re-layouts, body(): jnp.stack([query_grad.reshape(group_rows, local_width), key_grad.reshape(...  42.9 us
    psum x1, blocking collectives, body(): lax.psum((first_gain_grad, first_shift_grad, second_gain_grad, second_shi...  40.2 us
  transfers between devices with their start and end apart: 19, of which 15 were waited for; matrix products, arithmetic and copies ran while one was open for 25% of the time, Pallas kernels for 0%

profile of v1, /device:TPU:0, one launch (start us, length us, event | category | flops | bytes accessed | tf_op | source)
XLA Modules:
  0.0 1547.3 jit_solution(7847326728689312768)
XLA Ops:
  19.4 9.5 collective-permute-done.1
  32.5 17.3 %collective-permute-done.2 = bf16[3,256,512]{2,1,0:T(8,128)(2,1)} collective-permute-done((bf16[3,256,512]{2,1,0:T(8,128)(2,1)S(1)}, bf16[3,256,512]{2,1,0:T(8,128)(2,1)}, u32[]{:S(2)}, u32[]{:S(2)}) %collective-permute-start.2) | collective-permute-done | bytes 786464 | tf_op jit(solution)/shard_map/ppermute | solution.py:18
  56.4 68.6 %collective-permute-done.3 = bf16[3,512,512]{2,1,0:T(8,128)(2,1)} collective-permute-done((bf16[3,512,512]{2,1,0:T(8,128)(2,1)}, bf16[3,512,512]{2,1,0:T(8,128)(2,1)}, u32[]{:S(2)}, u32[]{:S(2)}) %collective-permute-start.3) | collective-permute-done | bytes 1572896 | tf_op jit(solution)/shard_map/ppermute | solution.py:18
  125.0 16.3 %convolution_bitcast_fusion = f32[3,2560,512]{1,2,0:T(8,128)} fusion(bf16[2560,1024]{1,0:T(8,128)(2,1)} %all-gather.8.cloned.1.call-done, bf16[3,512,512]{2,1,0:T(8,128)(2,1)} %collective-permute-done.3, bf16[3,512,512]{2,1,0:T(8,128)(2,1)} %maximum_select_fusion.1, pred[]{:T(512)S(6)} %eq.16), kind=kOutput, calls=%fused_computation.23 | convolution fusion | flops 8067219456 | bytes 24117248 | tf_op jit(solution)/shard_map/xz,ezi->exi/dot_general | solution.py:98
  145.6 8.8 fusion.64
  154.4 5.9 convert_element_type.127
  160.3 7.3 squeeze.7
  167.6 7.3 squeeze.8
  175.0 16.5 %fusion.13 = (f32[8,8,320]{2,1,0:T(8,128)S(1)}, f32[8,8,320,320]{2,3,1,0:T(8,128)}) fusion(pred[8,320]{1,0:T(8,128)(4,1)S(1)} %iota_compare_fusion, bf16[8,320,8,64]{1,0,3,2:T(8,128)(2,1)} %convert_element_type.127, f32[8,320,8,64]{1,0,3,2:T(8,128)} %squeeze.8, f32[8,64]{1,0:T(8,128)S(1)} %add.156), kind=kOutput, calls=%fused_computation.22 | convolution fusion | flops 861122560 | bytes 34165248 | tf_op jit(solution)/shard_map/bqhe,bkhe->bhqk/dot_general | solution.py:57
  191.5 14.2 fusion
  205.7 17.5 %convert_bitcast_fusion.2 = bf16[8,320,8,64]{1,3,2,0:T(8,128)(2,1)} fusion(f32[8,8,320]{2,1,0:T(8,128)S(1)} %fusion, f32[8,8,320]{2,1,0:T(8,128)S(1)} %get-tuple-element.91, f32[8,8,320,320]{2,3,1,0:T(8,128)} %get-tuple-element.92, pred[8,320]{1,0:T(8,128)(4,1)S(1)} %iota_compare_fusion, f32[8,320,8,64]{1,0,3,2:T(8,128)} %squeeze.7, f32[8,64]{1,0:T(8,128)S(1)} %add.152), kind=kOutput, calls=%fused_computation.72 | convolution fusion | flops 875560960 | bytes 34247168 | tf_op jit(solution)/shard_map/bhqk,bkhe->bqhe/dot_general | solution.py:113
  234.6 8.8 fusion.65
  244.2 121.9 %reduce-scatter.8.cloned.1.call-done = f32[1280,1024]{1,0:T(8,128)} async-done(((f32[2560,1024]{1,0:T(8,128)}), f32[1280,1024]{1,0:T(8,128)}) %reduce-scatter.8.cloned.1.call-update) | async-done | bytes 5242896 | tf_op jit(solution)/shard_map/reduce_scatter | solution.py:38
  374.6 44.1 %all-gather.14.cloned.1.call-done = bf16[1024,2048]{1,0:T(8,128)(2,1)} async-done(((bf16[64,2048]{1,0:T(8,128)(2,1)}), bf16[1024,2048]{1,0:T(8,128)(2,1)}) %all-gather.14.cloned.1.call-update) | async-done | bytes 4194320 | tf_op jit(solution)/shard_map/all_gather | solution.py:50
  418.7 69.1 %all-gather.12.cloned.1.call-done = bf16[2560,1024]{1,0:T(8,128)(2,1)} async-done(((bf16[1280,1024]{1,0:T(8,128)(2,1)}), bf16[2560,1024]{1,0:T(8,128)(2,1)}) %all-gather.12.cloned.1.call-update) | async-done | bytes 5242896 | tf_op jit(solution)/shard_map/all_gather | solution.py:34
  487.8 23.8 %multiply_convert_fusion.1 = (bf16[2560,2048]{1,0:T(8,128)(2,1)}, f32[2560,2048]{1,0:T(8,128)}) fusion(f32[2048]{0:T(1024)S(1)} %copy-done.42, bf16[2560,1024]{1,0:T(8,128)(2,1)} %all-gather.12.cloned.1.call-done, bf16[1024,2048]{1,0:T(8,128)(2,1)} %all-gather.14.cloned.1.call-done), kind=kOutput, calls=%fused_computation.18 | convolution fusion | flops 10789847040 | bytes 40902656 | tf_op jit(solution)/shard_map/dot_general | solution.py:126
  511.6 28.8 %all-gather.16.cloned.1.call-done = bf16[1024,2048]{1,0:T(8,128)(2,1)} async-done(((bf16[64,2048]{1,0:T(8,128)(2,1)}), bf16[1024,2048]{1,0:T(8,128)(2,1)}) %all-gather.16.cloned.1.call-update) | async-done | bytes 4194320 | tf_op jit(solution)/shard_map/all_gather | solution.py:51
  540.4 16.6 %fusion.66 = f32[2560,1024]{1,0:T(8,128)} fusion(bf16[2560,2048]{1,0:T(8,128)(2,1)} %get-tuple-element.93, bf16[1024,2048]{1,0:T(8,128)(2,1)} %all-gather.16.cloned.1.call-done), kind=kOutput, calls=%fused_computation.117 | convolution fusion | flops 10737418240 | bytes 25165824 | tf_op jit(solution)/shard_map/rf,df->rd/dot_general | solution.py:129
  559.1 118.4 %reduce-scatter.10.cloned.1.call-done = f32[1280,1024]{1,0:T(8,128)} async-done(((f32[2560,1024]{1,0:T(8,128)}), f32[1280,1024]{1,0:T(8,128)}) %reduce-scatter.10.cloned.1.call-update) | async-done | bytes 5242896 | tf_op jit(solution)/shard_map/reduce_scatter | solution.py:38
  677.5 6.3 fusion.58
  691.6 68.7 %all-gather.18.cloned.1.call-done = bf16[2560,1024]{1,0:T(8,128)(2,1)} async-done(((bf16[1280,1024]{1,0:T(8,128)(2,1)}), bf16[2560,1024]{1,0:T(8,128)(2,1)}) %all-gather.18.cloned.1.call-update) | async-done | bytes 5242896 | tf_op jit(solution)/shard_map/all_gather | solution.py:34
  760.2 28.8 %convert_reduce_fusion = (f32[2048]{0:T(1024)}, bf16[2560,2048]{1,0:T(8,128)(2,1)S(1)}) fusion(f32[2560,2048]{1,0:T(8,128)} %get-tuple-element.94, f32[2048]{0:T(1024)S(1)} %copy-done.42, bf16[2560,1024]{1,0:T(8,128)(2,1)} %all-gather.18.cloned.1.call-done, bf16[1024,2048]{1,0:T(8,128)(2,1)} %all-gather.16.cloned.1.call-done), kind=kOutput, calls=%fused_computation.17 | convolution fusion | flops 10858002432 | bytes 40910848 | tf_op jit(solution)/shard_map/dot_general | solution.py:138
  792.9 14.3 fusion.67
  807.3 122.0 %reduce-scatter.12.cloned.1.call-done = f32[1280,1024]{1,0:T(8,128)} async-done(((f32[2560,1024]{1,0:T(8,128)}), f32[1280,1024]{1,0:T(8,128)}) %reduce-scatter.12.cloned.1.call-update) | async-done | bytes 5242896 | tf_op jit(solution)/shard_map/reduce_scatter | solution.py:38
  929.3 5.8 multiply_reduce_fusion.1
  944.5 17.1 %convolution_convert_fusion.1 = bf16[1024,2048]{1,0:T(8,128)(2,1)} fusion(bf16[2560,1024]{1,0:T(8,128)(2,1)} %all-gather.18.cloned.1.call-done, bf16[2560,2048]{1,0:T(8,128)(2,1)} %get-tuple-element.93), kind=kOutput, calls=%fused_computation.65 | convolution fusion | flops 10739515392 | bytes 19922944 | tf_op jit(solution)/shard_map/rd,rf->df/dot_general | solution.py:139
  961.8 16.9 %convolution_convert_fusion.2 = bf16[1024,2048]{1,0:T(8,128)(2,1)} fusion(bf16[2560,1024]{1,0:T(8,128)(2,1)} %all-gather.12.cloned.1.call-done, bf16[2560,2048]{1,0:T(8,128)(2,1)} %copy-done.46), kind=kOutput, calls=%fused_computation.66 | convolution fusion | flops 10739515392 | bytes 19922944 | tf_op jit(solution)/shard_map/rd,rf->df/dot_general | solution.py:142
  978.7 34.5 %all-gather.20.cloned.1.call-done = bf16[2560,1024]{1,0:T(8,128)(2,1)} async-done(((bf16[1280,1024]{1,0:T(8,128)(2,1)}), bf16[2560,1024]{1,0:T(8,128)(2,1)}) %all-gather.20.cloned.1.call-update) | async-done | bytes 5242896 | tf_op jit(solution)/shard_map/all_gather | solution.py:34
  1023.8 5.9 copy.71
  1029.8 32.4 %multiply_reduce_fusion = (f32[8,8,320]{2,1,0:T(8,128)S(1)}, f32[8,8,320,320]{2,3,1,0:T(8,128)}) fusion(f32[8,8,320]{2,1,0:T(8,128)S(1)} %log_add_fusion, f32[8,8,320,320]{2,3,1,0:T(8,128)} %get-tuple-element.92, pred[8,320]{1,0:T(8,128)(4,1)S(1)} %iota_compare_fusion, bf16[8,320,8,64]{1,3,2,0:T(8,128)(2,1)S(1)} %copy.71, f32[8,320,8,64]{1,0,3,2:T(8,128)} %squeeze.7, ...), kind=kOutput, calls=%fused_computation.1 | convolution fusion | flops 874229760 | bytes 60461568 | tf_op jit(solution)/shard_map/bqhe,bkhe->bhqk/dot_general | solution.py:165
  1062.1 26.6 %multiply_convert_fusion = bf16[8,8,320,320]{2,3,1,0:T(8,128)(2,1)} fusion(f32[8,8,320,320]{2,3,1,0:T(8,128)} %get-tuple-element.96, f32[8,8,320]{2,1,0:T(8,128)S(1)} %get-tuple-element.95, f32[8,8,320]{2,1,0:T(8,128)S(1)} %log_add_fusion, f32[8,8,320,320]{2,3,1,0:T(8,128)} %get-tuple-element.92, pred[8,320]{1,0:T(8,128)(4,1)S(1)} %iota_compare_fusion), kind=kLoop, calls=%fused_computation | loop fusion | flops 39321600 | bytes 65702400 | tf_op jit(solution)/shard_map/convert_element_type | solution.py:171
  1088.7 15.1 convert_reduce_fusion.2
  1103.8 6.8 copy.94
  1110.6 8.1 reshape.161
  1118.7 10.4 fusion.32
  1134.1 8.1 reshape.160
  1142.2 10.5 convert_reduce_fusion.3
  1152.7 6.7 copy.92
  1159.4 8.0 reshape.159
  1173.3 10.8 convert_bitcast_fusion
  1189.9 7.2 convolution_convert_fusion.3
  1197.2 16.1 %convolution_bitcast_fusion.1 = f32[2560,1024]{1,0:T(8,128)} fusion(bf16[3,2560,512]{2,1,0:T(8,128)(2,1)} %copy-done.14, bf16[3,512,512]{2,1,0:T(8,128)(2,1)} %collective-permute-done.3, bf16[3,512,512]{2,1,0:T(8,128)(2,1)} %maximum_select_fusion.1, pred[]{:T(512)S(6)} %eq.16), kind=kOutput, calls=%fused_computation.33 | convolution fusion | flops 8067219456 | bytes 21495808 | tf_op jit(solution)/shard_map/mex,mwx->ew/dot_general | solution.py:200
  1218.9 61.5 %all-reduce.2 = (f32[2,512]{1,0:T(2,128)}, f32[2048]{0:T(1024)}) all-reduce(f32[2,512]{1,0:T(2,128)S(1)} %pad_maximum_fusion, f32[2048]{0:T(1024)S(1)} %copy-done.35), channel_id=1, replica_groups=mesh['dp'=16,'tensor'=2] {'dp'}, use_global_device_ids=true, to_apply=%region_25.26 | all-reduce | flops 3072 | bytes 24576 | tf_op jit(solution)/shard_map/psum | solution.py:225
  1280.4 21.1 %all-reduce.5.cloned.1.call-done = bf16[3,1024,512]{2,0,1:T(4,128)(2,1)} async-done(((bf16[3,1024,512]{2,0,1:T(4,128)(2,1)}), bf16[3,1024,512]{2,0,1:T(4,128)(2,1)}) %all-reduce.5.cloned.1.call-update) | async-done | bytes 3145744
  1303.4 58.4 %reduce-scatter.16.cloned.1.call-done = bf16[64,512]{1,0:T(8,128)(2,1)} async-done(((bf16[1024,512]{1,0:T(8,128)(2,1)}), bf16[64,512]{1,0:T(8,128)(2,1)}) %reduce-scatter.16.cloned.1.call-update) | async-done | bytes 65552 | tf_op jit(solution)/shard_map/reduce_scatter | solution.py:213
  1363.3 121.6 %reduce-scatter.14.cloned.1.call-done = f32[1280,1024]{1,0:T(8,128)} async-done(((f32[2560,1024]{1,0:T(8,128)}), f32[1280,1024]{1,0:T(8,128)}) %reduce-scatter.14.cloned.1.call-update) | async-done | bytes 5242896 | tf_op jit(solution)/shard_map/reduce_scatter | solution.py:38
  1492.0 40.2 %all-reduce.1 = (f32[]{:T(128)}, f32[1024]{0:T(1024)}, f32[1024]{0:T(1024)}, f32[1024]{0:T(1024)}, f32[1024]{0:T(1024)}, /*index=5*/f32[1024]{0:T(1024)}, f32[1024]{0:T(1024)}) all-reduce(f32[]{:T(128)} %get-tuple-element.90, f32[1024]{0:T(1024)S(1)} %get-tuple-element.62, ...), channel_id=1, replica_groups=mesh['dp'=16,'tensor'=2] {'dp','tensor'}, use_global_device_ids=true, to_apply=%region_9.10 | all-reduce | flops 6145 | bytes 49160 | tf_op jit(solution)/shard_map/psum | solution.py:226
  1532.9 6.5 add_add_fusion.2
  (190 shorter events, 112.4 us)
Async XLA Ops:
  7.2 5.1 copy-start.1
  7.2 5.1 copy-start.28
  7.2 5.1 copy-start.36
  7.2 117.8 %all-gather.8.cloned.1.call-start = ((), (), s32[]{:S(2)}) async-start(), calls=%async_computation.7 | async-start | bytes 7864320 | tf_op jit(solution)/shard_map/all_gather | solution.py:34
  9.6 5.1 copy-start.21
  14.6 41.4 %copy-start.40 = (f32[2,512]{1,0:T(2,128)S(1)}, f32[2,512]{1,0:T(2,128)}, u32[]{:S(2)}) copy-start(f32[2,512]{1,0:T(2,128)} %param.21) | copy-start | bytes 12292
  14.6 41.6 %copy-start.43 = (s32[128]{0:T(128)S(1)}, s32[128]{0:T(128)}, u32[]{:S(2)}) copy-start(s32[128]{0:T(128)} %param.17) | copy-start | bytes 1540
  14.6 219.9 %all-gather.10.cloned.1.call-start = ((), (), s32[]{:S(2)}) async-start(), calls=%async_computation.8 | async-start | bytes 1114112 | tf_op jit(solution)/shard_map/all_gather | solution.py:44
  14.7 1.6 collective-permute-start
  16.4 12.4 collective-permute-start.1
  30.6 19.2 %collective-permute-start.2 = (bf16[3,256,512]{2,1,0:T(8,128)(2,1)S(1)}, bf16[3,256,512]{2,1,0:T(8,128)(2,1)}, u32[]{:S(2)}, u32[]{:S(2)}) collective-permute-start(bf16[3,256,512]{2,1,0:T(8,128)(2,1)S(1)} %maximum_select_fusion.2), channel_id=1, source_target_pairs={{0,8},{2,10},{4,12},{6,14},{8,0},{10,2},{12,4},{14,6},{16,24},{18,... | collective-permute-start | bytes 2359304 | tf_op jit(solution)/shard_map/ppermute | solution.py:18
  52.9 72.0 %collective-permute-start.3 = (bf16[3,512,512]{2,1,0:T(8,128)(2,1)}, bf16[3,512,512]{2,1,0:T(8,128)(2,1)}, u32[]{:S(2)}, u32[]{:S(2)}) collective-permute-start(bf16[3,512,512]{2,1,0:T(8,128)(2,1)} %maximum_select_fusion.1), channel_id=1, source_target_pairs={{0,16},{2,18},{4,20},{6,22},{8,24},{10,26},{12,28},{14,30},{16,0},... | collective-permute-start | bytes 4718600 | tf_op jit(solution)/shard_map/ppermute | solution.py:18
  55.4 310.7 %reduce-scatter.8.cloned.1.call-start = ((), (), s32[]{:S(2)}) async-start(), calls=%async_computation.9 | async-start | bytes 15728640 | tf_op jit(solution)/shard_map/reduce_scatter | solution.py:38
  56.1 149.6 %copy-start.24 = (f32[8,64]{1,0:T(8,128)}, f32[8,64]{1,0:T(8,128)S(1)}, u32[]{:S(2)}) copy-start(f32[8,64]{1,0:T(8,128)S(1)} %add.152) | copy-start | bytes 6148
  56.2 118.7 %copy-start.19 = (f32[8,64]{1,0:T(8,128)}, f32[8,64]{1,0:T(8,128)S(1)}, u32[]{:S(2)}) copy-start(f32[8,64]{1,0:T(8,128)S(1)} %add.156) | copy-start | bytes 6148
  191.5 14.3 copy-start.12
  205.7 17.5 %copy-start.15 = (f32[8,8,320]{2,1,0:T(8,128)}, f32[8,8,320]{2,1,0:T(8,128)S(1)}, u32[]{:S(2)}) copy-start(f32[8,8,320]{2,1,0:T(8,128)S(1)} %fusion) | copy-start | bytes 245764
  243.4 122.7 %copy-start.37 = (f32[1024]{0:T(1024)S(1)}, f32[1024]{0:T(1024)}, u32[]{:S(2)}) copy-start(f32[1024]{0:T(1024)} %param.23) | copy-start | bytes 12292
  243.4 175.3 %all-gather.14.cloned.1.call-start = ((), (), s32[]{:S(2)}) async-start(), calls=%async_computation.11 | async-start | bytes 4456448 | tf_op jit(solution)/shard_map/all_gather | solution.py:50
  244.0 243.8 %all-gather.12.cloned.1.call-start = ((), (), s32[]{:S(2)}) async-start(), calls=%async_computation.10 | async-start | bytes 7864320 | tf_op jit(solution)/shard_map/all_gather | solution.py:34
  371.7 116.1 %copy-start.42 = (f32[2048]{0:T(1024)S(1)}, f32[2048]{0:T(1024)}, u32[]{:S(2)}) copy-start(f32[2048]{0:T(1024)} %param.27) | copy-start | bytes 24580
  374.0 166.4 %all-gather.16.cloned.1.call-start = ((), (), s32[]{:S(2)}) async-start(), calls=%async_computation.12 | async-start | bytes 4456448 | tf_op jit(solution)/shard_map/all_gather | solution.py:51
  374.5 303.0 %reduce-scatter.10.cloned.1.call-start = ((), (), s32[]{:S(2)}) async-start(), calls=%async_computation.13 | async-start | bytes 15728640 | tf_op jit(solution)/shard_map/reduce_scatter | solution.py:38
  557.0 120.5 %copy-start.39 = (f32[1024]{0:T(1024)S(1)}, f32[1024]{0:T(1024)}, u32[]{:S(2)}) copy-start(f32[1024]{0:T(1024)} %param.29) | copy-start | bytes 12292
  557.0 203.2 %all-gather.18.cloned.1.call-start = ((), (), s32[]{:S(2)}) async-start(), calls=%async_computation.14 | async-start | bytes 7864320 | tf_op jit(solution)/shard_map/all_gather | solution.py:34
  559.1 124.7 %copy-start.10 = (bf16[1280,1024]{1,0:T(8,128)(2,1)S(1)}, bf16[1280,1024]{1,0:T(8,128)(2,1)}, u32[]{:S(2)}) copy-start(bf16[1280,1024]{1,0:T(8,128)(2,1)} %param.16) | copy-start | bytes 7864324
  691.5 237.7 %reduce-scatter.12.cloned.1.call-start = ((), (), s32[]{:S(2)}) async-start(), calls=%async_computation.15 | async-start | bytes 15728640 | tf_op jit(solution)/shard_map/reduce_scatter | solution.py:38
  760.2 32.7 %copy-start.41 = (bf16[1024,2048]{1,0:T(8,128)(2,1)S(1)}, bf16[1024,2048]{1,0:T(8,128)(2,1)}, u32[]{:S(2)}) copy-start(bf16[1024,2048]{1,0:T(8,128)(2,1)} %all-gather.14.cloned.1.call-done) | copy-start | bytes 12582916
  807.2 205.9 %all-gather.20.cloned.1.call-start = ((), (), s32[]{:S(2)}) async-start(), calls=%async_computation.16 | async-start | bytes 7864320 | tf_op jit(solution)/shard_map/all_gather | solution.py:34
  929.3 5.8 copy-start.7
  929.3 9.7 slice-start
  944.5 17.2 %copy-start.13 = (f32[8,8,320]{2,1,0:T(8,128)S(1)}, f32[8,8,320]{2,1,0:T(8,128)}, u32[]{:S(2)}) copy-start(f32[8,8,320]{2,1,0:T(8,128)} %copy-done.12) | copy-start | bytes 245764
  944.5 17.2 %copy-start.16 = (f32[8,8,320]{2,1,0:T(8,128)S(1)}, f32[8,8,320]{2,1,0:T(8,128)}, u32[]{:S(2)}) copy-start(f32[8,8,320]{2,1,0:T(8,128)} %copy-done.15) | copy-start | bytes 245764
  944.5 270.7 %reduce-scatter.20.cloned.1.call-start = ((), (), s32[]{:S(2)}) async-start(), calls=%async_computation.20 | async-start | bytes 4456448 | tf_op jit(solution)/shard_map/reduce_scatter | solution.py:221
  961.7 255.3 %reduce-scatter.18.cloned.1.call-start = ((), (), s32[]{:S(2)}) async-start(), calls=%async_computation.19 | async-start | bytes 4456448 | tf_op jit(solution)/shard_map/reduce_scatter | solution.py:218
  978.7 322.9 %all-reduce.5.cloned.1.call-start = ((), (), s32[]{:S(2)}) async-start(), calls=%async_computation.21 | async-start | bytes 8388608
  1023.8 5.9 copy-start.25
  1110.6 8.1 copy-start.20
  1134.1 8.1 copy-start.6
  1159.4 10.1 copy-start.9
  1189.8 172.0 %reduce-scatter.16.cloned.1.call-start = ((), (), s32[]{:S(2)}) async-start(), calls=%async_computation.18 | async-start | bytes 1114112 | tf_op jit(solution)/shard_map/reduce_scatter | solution.py:213
  1197.1 287.8 %reduce-scatter.14.cloned.1.call-start = ((), (), s32[]{:S(2)}) async-start(), calls=%async_computation.17 | async-start | bytes 15728640 | tf_op jit(solution)/shard_map/reduce_scatter | solution.py:38
  1213.2 5.7 copy-start.35
  1213.2 271.6 %copy-start.2 = (bf16[1280,1024]{1,0:T(8,128)(2,1)S(1)}, bf16[1280,1024]{1,0:T(8,128)(2,1)}, u32[]{:S(2)}) copy-start(bf16[1280,1024]{1,0:T(8,128)(2,1)} %param.15) | copy-start | bytes 7864324
  1213.3 271.6 %copy-start.18 = (f32[1280]{0:T(1024)S(1)}, f32[1280]{0:T(1024)}, u32[]{:S(2)}) copy-start(f32[1280]{0:T(1024)} %copy-done.17) | copy-start | bytes 15364
  1213.3 271.6 %copy-start.29 = (f32[1024]{0:T(1024)S(1)}, f32[1024]{0:T(1024)}, u32[]{:S(2)}) copy-start(f32[1024]{0:T(1024)} %param.18) | copy-start | bytes 12292
  1216.9 271.8 %copy-start.27 = (f32[1280]{0:T(1024)S(1)}, f32[1280]{0:T(1024)}, u32[]{:S(2)}) copy-start(f32[1280]{0:T(1024)} %copy-done.26) | copy-start | bytes 15364
  1216.9 271.9 %copy-start.23 = (f32[1280]{0:T(1024)S(1)}, f32[1280]{0:T(1024)}, u32[]{:S(2)}) copy-start(f32[1280]{0:T(1024)} %copy-done.22) | copy-start | bytes 15364
  (20 other events, 54.9 us)
Sparse Core Ops, SparseCore 0:
  14.8 71.2 all-gather.7
  88.2 55.3 all-gather.9
  243.5 122.5 reduce-scatter.7
  368.1 50.5 all-gather.13
  420.7 67.0 all-gather.11
  489.8 50.5 all-gather.15
  557.1 120.3 reduce-scatter.9
  691.6 68.5 all-gather.17
  807.4 121.8 reduce-scatter.11
  944.6 68.5 all-gather.19
  1017.0 72.3 reduce-scatter.19
  1093.6 71.8 reduce-scatter.17
  1190.0 111.5 all-reduce.4
  1305.5 56.2 reduce-scatter.15
  1363.9 120.8 reduce-scatter.13
